TPU v7x, 1024 devices: a whole 4x4x32 slice. The times are simulated.
1024 devices in a mesh: node: 16 (over x, y), local: 64 (over z, core).
Axes of the slice: x: 4, y: 4, z: 32, core: 2. Of those that a mesh axis runs over, the one named last changes fastest.
Arguments:
- grad_out: bfloat16 [8192, 7168], P(('node', 'local')), may hold values from -6 to 6
- inputs: bfloat16 [8192, 7168], P(('node', 'local')), may hold values from -6 to 6
- group_ids: int32 [8192, 4], P(('node', 'local')), may hold values from 0 to 15, all different within a row; in each aligned block of 8 rows (0 to 7, 8 to 15, ...) at most 4 rows name the same one
- pair_code: int32 [8192, 4], P(('node', 'local')), may hold values from 0 to 239
- combine: bfloat16 [8192, 8], P(('node', 'local')), may hold values from 0.19921875 to 1
- w_gate: bfloat16 [1024, 1792, 128], P(('node', 'local')), may hold values from -0.0625 to 0.0625
- w_up: bfloat16 [1024, 1792, 128], P(('node', 'local')), may hold values from -0.0625 to 0.0625
- w_down: bfloat16 [1024, 128, 1792], P(('node', 'local')), may hold values from -0.125 to 0.125
Outputs:
- grad_inputs: bfloat16 [8192, 7168], P(('node', 'local'))
- grad_gate: bfloat16 [1024, 1792, 128], P(('node', 'local'))
- grad_up: bfloat16 [1024, 1792, 128], P(('node', 'local'))
- grad_down: bfloat16 [1024, 128, 1792], P(('node', 'local'))
Inputs may be any that keep to these rules, and one draw needn't show every extreme that they name: `group_ids`: each row names 4 different node groups; among the 8 rows of one device no group is named by more than 4 rows.
All inputs are finite; a program needn't handle non-finite values.
Results may differ from a plain program's by a relative error of at most 0.019.
Values may be sent and summed in bfloat16 or wider, within the bound.
A program may use at most 32 MiB of HBM per device.

v0:
```python
import jax
import jax.numpy as jnp
from jax import lax
from jax.sharding import PartitionSpec as P

TOP = 8
EXP_GROUP = 16
DQ = 4
CAPE = 4


def partner_2(block, axis, apart):
    count = lax.axis_size(axis)
    route = []
    for low in range(count):
        high = low | 1 << apart
        if high != low and high < count:
            route += [(low, high), (high, low)]
    return lax.ppermute(block, axis, route)


def expert_choice(group_ids, pair_code):
    first_pick = pair_code // (EXP_GROUP - 1)
    second_pick = (first_pick + 1 + pair_code % (EXP_GROUP - 1)) % EXP_GROUP
    pick_pairs = jnp.stack([first_pick, second_pick], axis=-1)
    chosen = group_ids[:, :, None] * EXP_GROUP + pick_pairs
    return chosen.reshape(group_ids.shape[0], TOP)


def window_weight(expert_ids, combine, node_count):
    targets = jnp.arange(node_count, dtype=jnp.int32) * EXP_GROUP
    matches = expert_ids[:, :, None] == targets[None, None, :]
    values = jnp.where(matches, combine.astype(jnp.float32)[:, :, None], jnp.float32(0.0))
    return jnp.sum(values, axis=1).astype(jnp.bfloat16)


def quarter_rows(slot_rows, local_count):
    capacity = slot_rows.shape[0]
    feature_part = slot_rows.shape[1] // DQ
    arranged = jnp.transpose(slot_rows.reshape(capacity, DQ, feature_part), (1, 0, 2))
    spread = jnp.broadcast_to(arranged[None], (local_count // DQ, DQ, capacity, feature_part))
    return spread.reshape(local_count, capacity, feature_part)


def on_device(grad_out, inputs, group_ids, pair_code, combine, w_gate, w_up, w_down):
    node_count = lax.axis_size("node")
    local_count = lax.axis_size("local")
    model_width = grad_out.shape[1]
    expert_ids = expert_choice(group_ids, pair_code)
    window = window_weight(expert_ids, combine, node_count)
    all_grad, all_input, all_weight = (
        lax.all_gather(grad_out, "node", axis=0, tiled=True),
        lax.all_gather(inputs, "node", axis=0, tiled=True),
        lax.all_gather(window, "node", axis=0, tiled=True),
    )
    cand_weight = lax.dynamic_slice_in_dim(all_weight, lax.axis_index("node"), 1, 1)[:, 0]
    is_live = (cand_weight > 0).astype(jnp.int32)
    live_rank = jnp.cumsum(is_live) - is_live
    slot_index = jnp.arange(CAPE, dtype=jnp.int32)
    chooser = ((is_live[None, :] == 1) & (live_rank[None, :] == slot_index[:, None])).astype(
        jnp.bfloat16
    )
    scaled = (cand_weight.astype(jnp.float32)[:, None] * all_grad.astype(jnp.float32)).astype(
        jnp.bfloat16
    )
    slot_grad = jnp.dot(chooser, scaled, preferred_element_type=jnp.float32).astype(jnp.bfloat16)
    slot_input = jnp.dot(chooser, all_input, preferred_element_type=jnp.float32).astype(
        jnp.bfloat16
    )
    expert_grad, expert_input = (
        lax.all_to_all(
            quarter_rows(slot_grad, local_count), "local", split_axis=0, concat_axis=0, tiled=True
        ),
        lax.all_to_all(
            quarter_rows(slot_input, local_count), "local", split_axis=0, concat_axis=0, tiled=True
        ),
    )
    feature_part = w_gate.shape[1]
    rows_grad = expert_grad.reshape(local_count * CAPE, feature_part)
    rows_input = expert_input.reshape(local_count * CAPE, feature_part)
    gate_weight = w_gate[0]
    up_weight = w_up[0]
    down_weight = w_down[0]
    contract_last = (((1,), (1,)), ((), ()))
    contract_first = (((0,), (0,)), ((), ()))
    gate_pre = jnp.dot(rows_input, gate_weight, preferred_element_type=jnp.float32)
    up_pre = jnp.dot(rows_input, up_weight, preferred_element_type=jnp.float32)
    hidden_grad = lax.dot_general(
        rows_grad, down_weight, contract_last, preferred_element_type=jnp.float32
    )
    for which_bit in range(DQ.bit_length() - 1):
        partner = (
            partner_2(gate_pre.astype(jnp.bfloat16), "local", which_bit).astype(gate_pre.dtype),
            partner_2(up_pre.astype(jnp.bfloat16), "local", which_bit).astype(up_pre.dtype),
            partner_2(hidden_grad.astype(jnp.bfloat16), "local", which_bit).astype(
                hidden_grad.dtype
            ),
        )
        gate_pre = gate_pre + partner[0]
        up_pre = up_pre + partner[1]
        hidden_grad = hidden_grad + partner[2]
    sigmoid_gate = jax.nn.sigmoid(gate_pre)
    activated = gate_pre * sigmoid_gate
    hidden = (activated * up_pre).astype(jnp.bfloat16)
    delta_up = (hidden_grad * activated).astype(jnp.bfloat16)
    delta_gate = (
        hidden_grad * up_pre * sigmoid_gate * (1.0 + gate_pre * (1.0 - sigmoid_gate))
    ).astype(jnp.bfloat16)
    grad_down = lax.dot_general(
        hidden, rows_grad, contract_first, preferred_element_type=jnp.float32
    ).astype(jnp.bfloat16)[None]
    grad_gate = lax.dot_general(
        rows_input, delta_gate, contract_first, preferred_element_type=jnp.float32
    ).astype(jnp.bfloat16)[None]
    grad_up = lax.dot_general(
        rows_input, delta_up, contract_first, preferred_element_type=jnp.float32
    ).astype(jnp.bfloat16)[None]
    input_part = lax.dot_general(
        delta_gate, gate_weight, contract_last, preferred_element_type=jnp.float32
    )
    input_part = input_part + lax.dot_general(
        delta_up, up_weight, contract_last, preferred_element_type=jnp.float32
    )
    input_part = input_part.astype(jnp.bfloat16).reshape(local_count, CAPE, feature_part)
    returned = lax.all_to_all(input_part, "local", split_axis=0, concat_axis=0, tiled=True)
    shard_groups = returned.reshape(local_count // DQ, DQ, CAPE, feature_part)
    summed = jnp.sum(shard_groups, axis=0, dtype=jnp.float32)
    relay_sum = jnp.transpose(summed, (1, 0, 2)).reshape(CAPE, model_width).astype(jnp.bfloat16)
    cand_sum = lax.dot_general(
        chooser, relay_sum, contract_first, preferred_element_type=jnp.float32
    )
    accumulated = lax.psum_scatter(
        cand_sum.astype(jnp.bfloat16), "node", scatter_dimension=0, tiled=True
    )
    return (accumulated, grad_gate, grad_up, grad_down)


def solution(mesh):
    in_specs = (
        P(("node", "local"), None),
        P(("node", "local"), None),
        P(("node", "local"), None),
        P(("node", "local"), None),
        P(("node", "local"), None),
        P(("node", "local"), None, None),
        P(("node", "local"), None, None),
        P(("node", "local"), None, None),
    )
    out_specs = (
        P(("node", "local"), None),
        P(("node", "local"), None, None),
        P(("node", "local"), None, None),
        P(("node", "local"), None, None),
    )
    return jax.shard_map(
        on_device, mesh=mesh, in_specs=in_specs, out_specs=out_specs, check_vma=False
    )
```

profile of v0, /device:TPU:1, one launch (start us, length us, event | category | flops | bytes accessed | tf_op | source)
XLA Modules:
  0.0 613.6 jit_solution(7635554697156288348)
XLA Ops:
  7.2 0.0 copy-start
  7.2 0.0 all-gather.3.cloned.1.call-start
  7.2 0.7 all-gather.3.cloned.1.call-update
  7.9 0.7 convert_element_type.108
  8.6 0.7 broadcast_multiply_fusion
  9.3 0.7 fusion.23
  10.0 0.1 copy.25
  10.1 0.1 select_reduce_fusion
  10.2 18.9 %all_gather.9 = bf16[128,16]{1,0:T(8,128)(2,1)S(1)} all-gather(bf16[8,16]{1,0:T(8,128)(2,1)S(1)} %select_reduce_fusion), channel_id=1, replica_groups=mesh['node'=16,'local'=64] {'node'}, dimensions={0}, use_global_device_ids=true | all-gather | bytes 4352 | tf_op jit(solution)/shard_map/all_gather | solution.py:54
  29.1 0.2 compare_reduce_fusion
  29.3 0.2 reduce-window.8
  29.5 0.2 convert_reduce_fusion
  29.7 0.2 subtract_reduce_fusion
  29.9 69.8 %all-gather.3.cloned.1.call-done = bf16[128,7168]{1,0:T(8,128)(2,1)} async-done(((bf16[8,7168]{1,0:T(8,128)(2,1)}), bf16[128,7168]{1,0:T(8,128)(2,1)}) %all-gather.3.cloned.1.call-update) | async-done | bytes 1835024 | tf_op jit(solution)/shard_map/all_gather | solution.py:52
  99.7 2.0 convolution_convert_fusion.2
  101.8 1.2 broadcast_in_dim.24
  102.9 24.9 %all-to-all-start = ((bf16[64,4,1792]{2,1,0:T(4,128)(2,1)}), bf16[64,4,1792]{2,1,0:T(4,128)(2,1)S(1)}, u32[]{:S(2)}, u32[]{:S(2)}) async-start(bf16[64,4,1792]{2,1,0:T(4,128)(2,1)} %bitcast.4), calls=%async_computation | async-start | bytes 1835008 | tf_op jit(solution)/shard_map/all_to_all | solution.py:71
  127.8 0.0 all-gather.5.cloned.1.call-start
  127.9 0.7 all-gather.5.cloned.1.call-update
  128.6 81.6 %all-gather.5.cloned.1.call-done = bf16[128,7168]{1,0:T(8,128)(2,1)} async-done(((bf16[8,7168]{1,0:T(8,128)(2,1)}), bf16[128,7168]{1,0:T(8,128)(2,1)}) %all-gather.5.cloned.1.call-update) | async-done | bytes 1835024 | tf_op jit(solution)/shard_map/all_gather | solution.py:53
  210.1 1.8 convolution_convert_fusion.1
  212.1 13.2 %all-to-all-done = bf16[64,4,1792]{2,1,0:T(4,128)(2,1)S(1)} async-done(((bf16[64,4,1792]{2,1,0:T(4,128)(2,1)}), bf16[64,4,1792]{2,1,0:T(4,128)(2,1)S(1)}, u32[]{:S(2)}, u32[]{:S(2)}) %all-to-all-start) | async-done | bytes 917536 | tf_op jit(solution)/shard_map/all_to_all | solution.py:71
  225.2 1.2 broadcast_in_dim.25
  226.4 12.0 %all-to-all-start.1 = ((bf16[64,4,1792]{2,1,0:T(4,128)(2,1)}), bf16[64,4,1792]{2,1,0:T(4,128)(2,1)S(1)}, u32[]{:S(2)}, u32[]{:S(2)}) async-start(bf16[64,4,1792]{2,1,0:T(4,128)(2,1)} %bitcast.7), calls=%async_computation.1 | async-start | bytes 1835008 | tf_op jit(solution)/shard_map/all_to_all | solution.py:74
  238.4 0.0 all-reduce.3.cloned.1.call-start
  238.4 0.2 reshape.96
  238.6 2.0 fusion.28
  240.7 2.4 collective-permute-start
  243.1 92.7 %all-to-all-done.1 = bf16[64,4,1792]{2,1,0:T(4,128)(2,1)S(1)} async-done(((bf16[64,4,1792]{2,1,0:T(4,128)(2,1)}), bf16[64,4,1792]{2,1,0:T(4,128)(2,1)S(1)}, u32[]{:S(2)}, u32[]{:S(2)}) %all-to-all-start.1) | async-done | bytes 917536 | tf_op jit(solution)/shard_map/all_to_all | solution.py:74
  335.8 0.2 reshape.99
  336.0 0.0 copy-start.1
  336.0 0.4 fusion.29
  336.4 4.4 collective-permute-start.4
  340.8 0.0 copy-done.1
  340.8 0.4 fusion.30
  341.2 1.9 collective-permute-start.2
  343.2 0.0 collective-permute-done
  343.2 0.0 copy-start.8
  343.2 2.2 collective-permute-start.1
  345.5 0.0 collective-permute-done.4
  345.5 0.0 copy-start.4
  345.5 3.0 collective-permute-start.5
  348.6 0.0 collective-permute-done.2
  348.6 2.2 collective-permute-start.3
  350.8 0.0 collective-permute-done.1
  350.9 0.0 collective-permute-done.5
  350.9 2.7 collective-permute-done.3
  353.6 1.0 multiply_convert_fusion.3
  354.6 0.0 copy-start.2
  354.6 0.4 fusion.5
  355.1 0.2 copy-done.2
  355.2 0.4 fusion
  355.6 1.1 reshape.100
  356.8 103.0 %all_to_all.15 = bf16[64,4,1792]{2,1,0:T(4,128)(2,1)S(1)} all-to-all(bf16[64,4,1792]{2,1,0:T(4,128)(2,1)} %reshape.100), channel_id=1, replica_groups=mesh['node'=16,'local'=64] {'local'}, dimensions={0} | all-to-all | bytes 1835008 | tf_op jit(solution)/shard_map/all_to_all | solution.py:125
  459.7 1.0 reduce
  460.8 2.8 convolution_convert_fusion
  463.6 0.0 all-reduce.3.cloned.1.call-update
  463.6 0.0 copy-start.12
  463.6 1.3 dynamic-slice
  465.6 1.2 fusion.2
  466.9 1.2 fusion.1
  468.1 1.1 fusion.3
  469.2 136.2 %all-reduce.3.cloned.1.call-done = bf16[128,7168]{1,0:T(8,128)(2,1)} async-done(((bf16[128,7168]{1,0:T(8,128)(2,1)}), bf16[128,7168]{1,0:T(8,128)(2,1)}) %all-reduce.3.cloned.1.call-update) | async-done | bytes 1835024
  605.5 1.6 constant_dynamic-slice_fusion
  (28 shorter events, 0.2 us)
Async XLA Ops:
  7.2 328.8 %copy-start = (bf16[1,1792,128]{2,1,0:T(8,128)(2,1)S(1)}, bf16[1,1792,128]{2,1,0:T(8,128)(2,1)}, u32[]{:S(2)}) copy-start(bf16[1,1792,128]{2,1,0:T(8,128)(2,1)} %param.13) | copy-start | bytes 1376260
  7.2 92.5 %all-gather.3.cloned.1.call-start = ((), (), s32[]{:S(2)}) async-start(), calls=%async_computation.3 | async-start | bytes 1949696 | tf_op jit(solution)/shard_map/all_gather | solution.py:52
  102.9 122.3 %all-to-all-start = ((bf16[64,4,1792]{2,1,0:T(4,128)(2,1)}), bf16[64,4,1792]{2,1,0:T(4,128)(2,1)S(1)}, u32[]{:S(2)}, u32[]{:S(2)}) async-start(bf16[64,4,1792]{2,1,0:T(4,128)(2,1)} %bitcast.4), calls=%async_computation | async-start | bytes 1835008 | tf_op jit(solution)/shard_map/all_to_all | solution.py:71
  127.8 82.3 %all-gather.5.cloned.1.call-start = ((), (), s32[]{:S(2)}) async-start(), calls=%async_computation.4 | async-start | bytes 1949696 | tf_op jit(solution)/shard_map/all_gather | solution.py:53
  226.4 109.4 %all-to-all-start.1 = ((bf16[64,4,1792]{2,1,0:T(4,128)(2,1)}), bf16[64,4,1792]{2,1,0:T(4,128)(2,1)S(1)}, u32[]{:S(2)}, u32[]{:S(2)}) async-start(bf16[64,4,1792]{2,1,0:T(4,128)(2,1)} %bitcast.7), calls=%async_computation.1 | async-start | bytes 1835008 | tf_op jit(solution)/shard_map/all_to_all | solution.py:74
  238.4 367.1 %all-reduce.3.cloned.1.call-start = ((), (), s32[]{:S(2)}) async-start(), calls=%async_computation.5 | async-start | bytes 3670016
  240.7 102.5 %collective-permute-start = (bf16[256,128]{1,0:T(8,128)(2,1)}, bf16[256,128]{1,0:T(8,128)(2,1)S(1)}, u32[]{:S(2)}, u32[]{:S(2)}) collective-permute-start(bf16[256,128]{1,0:T(8,128)(2,1)} %get-tuple-element.10), channel_id=1, source_target_pairs={{0,1},{1,0},{2,3},{3,2},{4,5},{5,4},{6,7},{7,6},{8,9},{9,8},{10,11... | collective-permute-start | bytes 196616 | tf_op jit(solution)/shard_map/ppermute | solution.py:19
  336.0 4.8 copy-start.1
  336.4 9.0 %collective-permute-start.4 = (bf16[256,128]{1,0:T(8,128)(2,1)S(1)}, bf16[256,128]{1,0:T(8,128)(2,1)S(1)}, u32[]{:S(2)}, u32[]{:S(2)}) collective-permute-start(bf16[256,128]{1,0:T(8,128)(2,1)S(1)} %get-tuple-element.12), channel_id=1, source_target_pairs={{0,1},{1,0},{2,3},{3,2},{4,5},{5,4},{6,7},{7,6},{8,9},{9,8},{10,11... | collective-permute-start | bytes 196616 | tf_op jit(solution)/shard_map/ppermute | solution.py:19
  341.2 7.3 %collective-permute-start.2 = (bf16[256,128]{1,0:T(8,128)(2,1)S(1)}, bf16[256,128]{1,0:T(8,128)(2,1)S(1)}, u32[]{:S(2)}, u32[]{:S(2)}) collective-permute-start(bf16[256,128]{1,0:T(8,128)(2,1)S(1)} %get-tuple-element.14), channel_id=1, source_target_pairs={{0,1},{1,0},{2,3},{3,2},{4,5},{5,4},{6,7},{7,6},{8,9},{9,8},{10,11... | collective-permute-start | bytes 196616 | tf_op jit(solution)/shard_map/ppermute | solution.py:19
  343.2 7.7 %copy-start.8 = (bf16[256,128]{1,0:T(8,128)(2,1)}, bf16[256,128]{1,0:T(8,128)(2,1)S(1)}, u32[]{:S(2)}) copy-start(bf16[256,128]{1,0:T(8,128)(2,1)S(1)} %collective-permute-done) | copy-start | bytes 196612
  343.2 7.6 %collective-permute-start.1 = (bf16[256,128]{1,0:T(8,128)(2,1)S(1)}, bf16[256,128]{1,0:T(8,128)(2,1)S(1)}, u32[]{:S(2)}, u32[]{:S(2)}) collective-permute-start(bf16[256,128]{1,0:T(8,128)(2,1)S(1)} %fusion.15), channel_id=1, source_target_pairs={{0,2},{2,0},{1,3},{3,1},{4,6},{6,4},{5,7},{7,5},{8,10},{10,8},{9,1... | collective-permute-start | bytes 196616 | tf_op jit(solution)/shard_map/ppermute | solution.py:19
  345.5 9.6 %copy-start.4 = (bf16[256,128]{1,0:T(8,128)(2,1)}, bf16[256,128]{1,0:T(8,128)(2,1)S(1)}, u32[]{:S(2)}) copy-start(bf16[256,128]{1,0:T(8,128)(2,1)S(1)} %collective-permute-done.4) | copy-start | bytes 196612
  345.5 5.4 collective-permute-start.5
  348.6 6.5 %copy-start.6 = (bf16[256,128]{1,0:T(8,128)(2,1)}, bf16[256,128]{1,0:T(8,128)(2,1)S(1)}, u32[]{:S(2)}) copy-start(bf16[256,128]{1,0:T(8,128)(2,1)S(1)} %collective-permute-done.2) | copy-start | bytes 196612
  348.6 5.0 collective-permute-start.3
  350.9 4.2 copy-start.9
  353.6 1.4 copy-start.11
  354.6 0.6 copy-start.2
  460.8 4.9 copy-start.3
  463.6 4.5 copy-start.5
  463.6 4.5 copy-start.7
  463.6 4.5 copy-start.10
  463.6 4.5 copy-start.12
Sparse Core Ops, SparseCore 0:
  12.2 87.4 all-gather.2
  132.9 77.2 all-gather.4
  463.7 141.7 all-reduce.2
where the time goes:
time: 615 us; the launch traced here: 614 us
  waiting for transfers between devices  398 us (65%)
  blocking collectives  122 us (20%)
  starting transfers between devices  53.2 us (9%)
  between operations  14.8 us (2%)
  matrix products  13.9 us (2%)
  local copies, waits for them, and re-layouts  7.18 us (1%)
    unnamed x4, waiting for transfers between devices  138 us
    all_to_all x1, blocking collectives, on_device(): lax.all_to_all(input_part, 'local', split_axis=0, concat_axis=0, tiled=True)  103 us
    all_to_all x1, waiting for transfers between devices, on_device(): lax.all_to_all(quarter_rows(slot_input, local_count), 'local', split_axis...  92.7 us
    all_gather x1, waiting for transfers between devices, on_device(): lax.all_gather(inputs, 'node', axis=0, tiled=True)  81.6 us
    all_gather x1, waiting for transfers between devices, on_device(): lax.all_gather(grad_out, 'node', axis=0, tiled=True)  69.8 us
    all_to_all x1, starting transfers between devices, on_device(): lax.all_to_all(quarter_rows(slot_grad, local_count), 'local', split_axis=...  24.9 us
    all_gather x1, blocking collectives, on_device(): lax.all_gather(window, 'node', axis=0, tiled=True)  18.9 us
    ppermute x6, starting transfers between devices, partner_2(): return lax.ppermute(block, axis, route)  16.2 us
  transfers between devices with their start and end apart: 11, of which 6 were waited for; matrix products, arithmetic and copies ran while one was open for 2% of the time, Pallas kernels for 0%

commit v1 on v0

v1 whole, which is shorter than its diff:
```python
import functools
import math

import jax
import jax.numpy as jnp
from jax import lax
from jax.experimental import pallas as pl
from jax.experimental.pallas import tpu as pltpu
from jax.sharding import PartitionSpec as P

EXP_GROUP = 16
DQ = 4
CAPE = 4
TOK = 8
ROWS = DQ * CAPE
LANES = 128
GROUPS = 16
LAG = 1
AHEAD = 4
AG_JUMP = (0, 0, 0, 0)
RS_JUMP = 3
MESH = pl.DeviceIdType.MESH
F32 = jnp.float32
BF16 = jnp.bfloat16


def iota(shape, dim):
    return lax.broadcasted_iota(jnp.int32, shape, dim)


def grid_of(rows, cols):
    return iota((rows, cols), 0), iota((rows, cols), 1)


def one(where):
    return jnp.where(where, 1.0, 0.0).astype(BF16)


def dot(a, b, contract=((1,), (0,))):
    return lax.dot_general(a, b, (contract, ((), ())), preferred_element_type=F32)


LAST = ((1,), (1,))
FIRST = ((0,), (0,))


class Route:
    def __init__(self, far, jump):
        self.far = far
        self.jump = jump if 1 < jump <= far else 0

    def parent(self, i):
        return 0 if i == self.jump else i - 1

    def children(self, p):
        return [i for i in range(1, self.far + 1) if self.parent(i) == p]

    def arrival(self, i):
        return i if not self.jump or i < self.jump else i - self.jump + 2

    def last(self):
        return max(self.arrival(i) for i in range(1, self.far + 1))


def pieces_of(half):
    tiles = half // LANES
    lead = (tiles + 1) // 2
    out = []
    for h in range(2):
        out.append((h, h * half, lead * LANES))
        if tiles > lead:
            out.append((h, h * half + lead * LANES, (tiles - lead) * LANES))
    return out


def kernel(
    nx, ny, nq,
    grad_ref, inp_ref, gid_ref, code_ref, comb_ref, wg_ref, wu_ref, wd_ref,
    fin, gg_ref, gu_ref, gd_ref,
    tok_out, tok, win, wts, packed, cnt, cnts, arrived, xs, dys, wgu,
    mine, part, quad_in, hgrad, hpart, hquad_in, hid, back,
    summed, leaves, relay, allrelay, fin_out,
    tok_send, tok_recv, win_send, win_recv, pack_send, pack_recv, cnt_send, cnt_recv,
    ag_send, ag_recv, mid_send, mid_recv, hid_send, hid_recv,
    rs_send, rs_recv, rel_send, rel_recv, fin_send, fin_recv,
):
    nodes = nx * ny
    feat = wg_ref.shape[0]
    hw = wg_ref.shape[1]
    half = feat // 2
    slots = nodes * ROWS
    to_right = nq // 2
    steps_of = (to_right, nq - 1 - to_right)
    me_n = lax.axis_index("node")
    me_l = lax.axis_index("local")
    quad = lax.div(me_l, DQ)
    b = lax.rem(me_l, DQ)
    my_x, my_y = lax.div(me_n, ny), lax.rem(me_n, ny)

    def quad_at(k):
        return (me_n, lax.rem(quad + (k + nq) % nq, nq) * DQ + b)

    ag_routes = [[Route(far, jump) for far in steps_of] for jump in AG_JUMP]
    rs_routes = [Route(far, RS_JUMP) for far in steps_of]
    apart = {1, nq - 1}
    for route in sum(ag_routes, rs_routes):
        if route.jump:
            apart |= {route.jump, nq - route.jump}
    offsets = [(dx, dy) for dx in range(nx) for dy in range(ny) if dx or dy]
    peers = range(len(offsets))
    mates = range(1, DQ)
    spans = [pl.ds(h * half, half) for h in range(2)]
    started = []

    def go(c):
        c.start()
        started.append(c)

    def node_at(dx, dy):
        return lax.rem(my_x + dx, nx) * ny + lax.rem(my_y + dy, ny)

    def node_to(k):
        dx, dy = offsets[k]
        return node_at(dx, dy)

    def node_from(k):
        dx, dy = offsets[k]
        return node_at(nx - dx, ny - dy)

    def mate(d):
        return lax.bitwise_xor(b, d)

    def in_quad(d):
        return (me_n, quad * DQ + mate(d))

    def copy(src, dst, send, recv, device):
        return pltpu.make_async_remote_copy(
            src_ref=src, dst_ref=dst, send_sem=send, recv_sem=recv,
            device_id=device, device_id_type=MESH,
        )

    barrier = pltpu.get_barrier_semaphore()
    greet = [(node_to(k), me_l) for k in peers] + [in_quad(d) for d in mates]
    greet += [quad_at(k) for k in sorted(apart)]
    for device in greet:
        pl.semaphore_signal(barrier, inc=1, device_id=device, device_id_type=MESH)

    for q in range(DQ):
        for h in range(2):
            at = slice(q * feat + h * half, q * feat + (h + 1) * half)
            tok_out[h, q] = jnp.concatenate(
                [inp_ref[:, at].astype(F32), grad_ref[:, at].astype(F32)], axis=0
            ).astype(BF16)
    chosen, top = gid_ref.shape[0], comb_ref.shape[1]
    code = code_ref[...]
    first = jnp.zeros_like(code)
    for m in range(1, EXP_GROUP):
        first = first + jnp.where(code >= m * (EXP_GROUP - 1), 1, 0)
    second = first + 1 + (code - (EXP_GROUP - 1) * first)
    second = jnp.where(second >= EXP_GROUP, second - EXP_GROUP, second)
    row, col = grid_of(chosen, top)
    comb = comb_ref[...]
    weight = jnp.where(first == 0, dot(one(col == 2 * row), comb, LAST), 0.0)
    weight = weight + jnp.where(second == 0, dot(one(col == 2 * row + 1), comb, LAST), 0.0)
    window = jnp.zeros((GROUPS, TOK), F32)
    for k in range(chosen):
        named = iota((GROUPS, TOK), 0) == gid_ref[k:k + 1, :]
        window = window + jnp.where(named, weight[k:k + 1, :], 0.0)
    row, col = grid_of(TOK, LANES)
    win[...] = dot(window.astype(BF16), one(row == col))

    pl.semaphore_wait(barrier, len(greet))

    def tok_copy(d, h, slot):
        return copy(
            tok_out.at[h, mate(d)], tok.at[h, slot], tok_send.at[h, d], tok_recv.at[h, d],
            in_quad(d),
        )

    def win_copy(d, slot):
        return copy(win, wts.at[slot], win_send.at[d], win_recv.at[d], in_quad(d))

    for d in mates:
        go(win_copy(d, b))
    for h in range(2):
        for d in mates:
            go(tok_copy(d, h, b))
        tok[h, b] = tok_out[h, b]
    wts[b] = win[...]

    cols = 2 * DQ * TOK
    row, col = grid_of(cols, cols)
    below = one((row >> 3 == col >> 3) & (row < col))
    row, col = grid_of(cols, slots)
    tally = one((((row >> 3) & 1) == 0) & (row >> 4 == (col >> 2) & 3) & (col >> 4 == me_n))
    row, col = grid_of(slots, GROUPS)
    of_group = one(row >> 4 == col)
    row, col = grid_of(GROUPS, slots)
    group_of = one(row == col >> 4)
    row, col = grid_of(slots, slots)
    before = one((row >> 4 < col >> 4) & ((row & 15) == (col & 15)))
    row, col = grid_of(slots, cols)
    own_base = one((row >> 4 == me_n) & ((row & 3) == 0) & (((row >> 2) & 3) == col >> 4))
    wgu[:, 0:hw] = wg_ref[...]
    wgu[:, hw:2 * hw] = wu_ref[...]

    for d in mates:
        win_copy(d, mate(d)).wait_recv()
    weights = jnp.zeros((GROUPS, cols), F32)
    row, col = grid_of(LANES, cols)
    for j in range(DQ):
        weights = weights + dot(wts[j].astype(BF16), one((row == (col & 7)) & (col >> 4 == j)))
    live = one(weights > 0)
    ranks = dot(live, below)
    cnt[...] = dot(live, tally).astype(BF16)

    def cnt_copy(k, slot):
        return copy(cnt, cnts.at[slot], cnt_send.at[k], cnt_recv.at[k], (node_to(k), me_l))

    def pack_copy(c, k, slot):
        return copy(
            packed.at[c, node_to(k)], arrived.at[c, slot], pack_send.at[c, k], pack_recv.at[c, k],
            (node_to(k), me_l),
        )

    w_at = dot(of_group, weights.astype(BF16))
    r_at = dot(of_group, ranks.astype(BF16))
    row, col = grid_of(slots, cols)
    fits = ((row >> 2) & 3) == col >> 4
    fits = fits & (r_at == (row & 3).astype(F32)) & (w_at > 0)
    is_grad = ((col >> 3) & 1) == 1
    picks = [
        one(fits & jnp.logical_not(is_grad)),
        jnp.where(fits & is_grad, w_at, 0.0).astype(BF16),
    ]

    def pack(c):
        a, h = c // 2, c % 2
        rows = dot(picks[a], tok[h].reshape(cols, half))
        packed[c] = rows.astype(BF16).reshape(nodes, ROWS, half)
        arrived[c, me_n] = packed[c, me_n]

    def pack_go(c):
        for k in peers:
            go(pack_copy(c, k, me_n))

    for d in mates:
        tok_copy(d, 0, mate(d)).wait_recv()
    pack(0)
    pack_go(0)
    for k in peers:
        go(cnt_copy(k, me_n))
    cnts[me_n] = cnt[...]
    for d in mates:
        tok_copy(d, 1, mate(d)).wait_recv()
    pack(1)
    for c in range(1, AHEAD):
        if c > 1:
            pack(c)
        pack_go(c)
    for c in range(max(2, AHEAD), 4):
        pack(c)

    for k in peers:
        cnt_copy(k, node_from(k)).wait_recv()
    counts = jnp.zeros((GROUPS, slots), F32)
    for m in range(nodes):
        counts = counts + cnts[m].astype(F32)
    begin = dot(counts.astype(BF16), before).astype(BF16)
    row, col = grid_of(ROWS, GROUPS)
    start = dot(one(col == me_n), begin)
    row, col = grid_of(ROWS, slots)
    merge = one(
        (row >> 2 == (col >> 2) & 3) & ((row & 3).astype(F32) == start + (col & 3).astype(F32))
    )
    place = jnp.where(weights > 0, ranks + dot(begin, own_base), 255.0)
    place = dot(place.astype(BF16), group_of, FIRST)
    row, col = grid_of(cols, slots)
    stands = (row >> 4 == (col >> 2) & 3) & (place == (col & 3).astype(F32))
    collect = [one(stands & (((row >> 3) & 1) == h)) for h in range(2)]

    rings = (xs, dys)

    def block(c, i):
        return rings[c // 2].at[pl.ds(i * ROWS, ROWS), spans[c % 2]]

    def place_of(way, i):
        return i if way == 0 else (nq - i) % nq

    def ag_copy(c, way, i):
        p = ag_routes[c][way].parent(i)
        src, dst = place_of(way, p), place_of(way, i)
        return copy(
            block(c, src), block(c, dst), ag_send.at[c, dst], ag_recv.at[c, dst],
            quad_at(i - p if way == 0 else p - i),
        )

    def ag_wait(c, way, i):
        dst = place_of(way, i)
        copy(
            block(c, dst), block(c, dst), ag_send.at[c, dst], ag_recv.at[c, dst], quad_at(1)
        ).wait_recv()

    share = nq * ROWS // DQ

    def rows_at(ref, owner, at, width):
        return ref.at[pl.ds(pl.multiple_of(owner * share, share), share), pl.ds(at, width)]

    def own_rows(ref):
        return ref[pl.ds(pl.multiple_of(b * share, share), share), :]

    def mid_copy(d):
        return copy(
            rows_at(part, mate(d), 0, 2 * hw), quad_in.at[d - 1],
            mid_send.at[0, d], mid_recv.at[0, d], in_quad(d),
        )

    def hgrad_copy(d):
        return copy(
            rows_at(hpart, mate(d), 0, hw), hquad_in.at[d - 1],
            mid_send.at[1, d], mid_recv.at[1, d], in_quad(d),
        )

    whole = set()

    def after_chunk(c):
        span = slice((c % 2) * half, (c % 2 + 1) * half)
        whole.add(c)
        a = c // 2
        if a == 0:
            total = dot(xs[:, span], wgu[span, :])
        else:
            total = dot(dys[:, span], wd_ref[:, span], LAST)
        both = {2 * a, 2 * a + 1} <= whole
        keep, send, move = ((mine, part, mid_copy), (hgrad, hpart, hgrad_copy))[a]
        if both:
            total = keep[...] + total
            send[...] = total.astype(BF16)
            for d in mates:
                go(move(d))
        keep[...] = total

    last = [max(route.last() for route in routes) for routes in ag_routes]
    for turn in range(max(last[c] + LAG * c for c in range(4)) + 1):
        for c in range(4):
            step = turn - LAG * c
            if step == 0:
                for k in peers:
                    pack_copy(c, k, node_from(k)).wait_recv()
                merged = dot(merge, arrived[c].reshape(slots, half)).astype(BF16)
                rings[c // 2][0:ROWS, (c % 2) * half:(c % 2 + 1) * half] = merged
                for way in range(2):
                    for i in reversed(ag_routes[c][way].children(0)):
                        go(ag_copy(c, way, i))
                if c + AHEAD < 4:
                    pack_go(c + AHEAD)
            for way in range(2):
                route = ag_routes[c][way]
                for i in range(route.far, 0, -1):
                    if route.arrival(i) == step:
                        ag_wait(c, way, i)
                        for j in route.children(i):
                            go(ag_copy(c, way, j))
            if step == last[c]:
                after_chunk(c)

    total = own_rows(mine)
    for d in mates:
        mid_copy(d).wait_recv()
        total = total + quad_in[d - 1].astype(F32)
    gate_pre, up_pre = total[:, :hw], total[:, hw:]
    sigmoid_gate = 1.0 / (1.0 + jnp.exp(-gate_pre))
    activated = gate_pre * sigmoid_gate
    slope = up_pre * sigmoid_gate * (1.0 + gate_pre * (1.0 - sigmoid_gate))
    hidden_grad = own_rows(hgrad)
    for d in mates:
        hgrad_copy(d).wait_recv()
        hidden_grad = hidden_grad + hquad_in[d - 1].astype(F32)
    hid[pl.ds(pl.multiple_of(b * share, share), share), :] = jnp.concatenate(
        [hidden_grad * slope, hidden_grad * activated, activated * up_pre], axis=1
    ).astype(BF16)

    def hid_copy(d, owner, i):
        at, width = ((0, 2 * hw), (2 * hw, hw))[i]
        return copy(
            rows_at(hid, b, at, width), rows_at(hid, owner, at, width),
            hid_send.at[i, d], hid_recv.at[i, d], in_quad(d),
        )

    for i in range(2):
        for d in mates:
            go(hid_copy(d, b, i))
    for d in mates:
        hid_copy(d, mate(d), 0).wait_recv()
    deltas = hid[:, 0:2 * hw]
    back[...] = dot(deltas, wgu[...], LAST)

    pieces = pieces_of(half)

    def rs_copy(way, i, p):
        route = rs_routes[way]
        _, at, width = pieces[p]
        span = pl.ds(at, width)
        src = summed.at[way, i + 1, :, span] if route.children(i) else leaf(way, i).at[:, span]
        k = i - route.parent(i)
        return copy(
            src, summed.at[way, i, :, span], rs_send.at[way, i - 1, p], rs_recv.at[way, i - 1, p],
            quad_at(-k if way == 0 else k),
        )

    def leaf(way, i):
        return leaves.at[way, 0 if i == rs_routes[way].far else 1]

    def own_block(way, i, span):
        at = place_of(way, i) * ROWS
        return back[at:at + ROWS, span]

    for step in range(to_right):
        for chain in range(2):
            for p, (_, at, width) in enumerate(pieces):
                span = slice(at, at + width)
                for way in range(2):
                    route = rs_routes[way]
                    i = (route.jump - 1 if chain else route.far) - step
                    if i < (1 if chain else max(route.jump, 1)):
                        continue
                    own = own_block(way, i, span)
                    if step == 0:
                        leaves[way, chain, :, span] = own.astype(BF16)
                    else:
                        rs_copy(way, i + 1, p).wait_recv()
                        summed[way, i + 1, :, span] = (
                            summed[way, i + 1, :, span].astype(F32) + own
                        ).astype(BF16)
                    go(rs_copy(way, i, p))

    def rel_copy(h, k, slot):
        return copy(
            relay.at[h], allrelay.at[h, slot], rel_send.at[h, k], rel_recv.at[h, k],
            (node_to(k), me_l),
        )

    for p, (h, at, width) in enumerate(pieces):
        span = slice(at, at + width)
        acc = back[0:ROWS, span]
        for way in (1, 0):
            for i in rs_routes[way].children(0):
                rs_copy(way, i, p).wait_recv()
                acc = acc + summed[way, i, :, span].astype(F32)
        relay[h, :, at - h * half:at - h * half + width] = acc.astype(BF16)
        if at + width == (h + 1) * half:
            for k in peers:
                go(rel_copy(h, k, me_n))

    allrelay[0, me_n] = relay[0]
    allrelay[1, me_n] = relay[1]
    grads = dot(xs[...], deltas, FIRST)
    gg_ref[...] = grads[:, :hw].astype(BF16)
    gu_ref[...] = grads[:, hw:].astype(BF16)
    for d in mates:
        hid_copy(d, mate(d), 1).wait_recv()
    gd_ref[...] = dot(hid[:, 2 * hw:3 * hw], dys[...], FIRST).astype(BF16)

    sums = jnp.zeros((cols, half), F32)
    for h in range(2):
        for k in peers:
            rel_copy(h, k, node_from(k)).wait_recv()
        sums = sums + dot(collect[h], allrelay[h].reshape(slots, half))
    fin_out[...] = sums.astype(BF16).reshape(DQ, 2 * TOK, half)

    def fin_copy(d, slot):
        return copy(
            fin_out.at[mate(d)], fin.at[slot], fin_send.at[d], fin_recv.at[d], in_quad(d)
        )

    for d in mates:
        go(fin_copy(d, b))
    fin[b] = fin_out[b]
    for d in mates:
        fin_copy(d, mate(d)).wait_recv()
    for c in started:
        c.wait_send()


def hand_on(fin, gg, gu, gd, gi_ref, gg_ref, gu_ref, gd_ref, gg_mid, gu_mid, gd_mid, sem):
    moves = ((gg, gg_mid, gg_ref), (gu, gu_mid, gu_ref), (gd, gd_mid, gd_ref))
    loads = [pltpu.make_async_copy(m[0], m[1], sem.at[0, i]) for i, m in enumerate(moves)]
    stores = [pltpu.make_async_copy(m[1], m[2], sem.at[1, i]) for i, m in enumerate(moves)]
    for c in loads:
        c.start()
    half = fin.shape[2]
    for q in range(DQ):
        got = fin[q].astype(F32)
        for h in range(2):
            at = (2 * q + h) * half
            gi_ref[:, at:at + half] = got[h * TOK:(h + 1) * TOK].astype(BF16)
    for load, store in zip(loads, stores):
        load.wait()
        store.start()
    for c in stores:
        c.wait()


def on_device(shape, grad_out, inputs, group_ids, pair_code, combine, w_gate, w_up, w_down):
    nodes, locals_ = shape
    nx = math.isqrt(nodes)
    ny = nodes // nx
    nq = locals_ // DQ
    feat, hw = w_gate.shape[1:]
    half = feat // 2
    width = grad_out.shape[1]
    ring = nq * ROWS
    slots = nodes * ROWS
    to_right = nq // 2
    pieces = len(pieces_of(half))
    dma = pltpu.SemaphoreType.DMA
    peers = nodes - 1
    operands = (
        grad_out, inputs, group_ids.T, pair_code.T, combine, w_gate[0], w_up[0], w_down[0]
    )
    outs = ((DQ, 2 * TOK, half), (feat, hw), (feat, hw), (hw, feat))

    def whole(dims):
        return pl.BlockSpec(dims, lambda i: (0,) * len(dims))

    hbm = pl.BlockSpec(memory_space=pl.ANY)
    results = pl.pallas_call(
        functools.partial(kernel, nx, ny, nq),
        grid=(1,),
        out_shape=tuple(jax.ShapeDtypeStruct(dims, BF16) for dims in outs),
        in_specs=[whole(o.shape) for o in operands],
        out_specs=tuple(whole(dims) for dims in outs),
        scratch_shapes=[
            pltpu.VMEM((2, DQ, 2 * TOK, half), BF16),
            pltpu.VMEM((2, DQ, 2 * TOK, half), BF16),
            pltpu.VMEM((GROUPS, LANES), F32),
            pltpu.VMEM((DQ, GROUPS, LANES), F32),
            pltpu.VMEM((4, nodes, ROWS, half), BF16),
            pltpu.VMEM((GROUPS, slots), BF16),
            pltpu.VMEM((nodes, GROUPS, slots), BF16),
            pltpu.VMEM((4, nodes, ROWS, half), BF16),
            pltpu.VMEM((ring, feat), BF16),
            pltpu.VMEM((ring, feat), BF16),
            pltpu.VMEM((feat, 2 * hw), BF16),
            pltpu.VMEM((ring, 2 * hw), F32),
            pltpu.VMEM((ring, 2 * hw), BF16),
            pltpu.VMEM((DQ - 1, ring // DQ, 2 * hw), BF16),
            pltpu.VMEM((ring, hw), F32),
            pltpu.VMEM((ring, hw), BF16),
            pltpu.VMEM((DQ - 1, ring // DQ, hw), BF16),
            pltpu.VMEM((ring, 3 * hw), BF16),
            pltpu.VMEM((ring, feat), F32),
            pltpu.VMEM((2, to_right + 1, ROWS, feat), BF16),
            pltpu.VMEM((2, 2, ROWS, feat), BF16),
            pltpu.VMEM((2, ROWS, half), BF16),
            pltpu.VMEM((2, nodes, ROWS, half), BF16),
            pltpu.VMEM((DQ, 2 * TOK, half), BF16),
            dma((2, DQ)), dma((2, DQ)), dma((DQ,)), dma((DQ,)),
            dma((4, peers)), dma((4, peers)), dma((peers,)), dma((peers,)),
            dma((4, nq)), dma((4, nq)),
            dma((2, DQ)), dma((2, DQ)), dma((2, DQ)), dma((2, DQ)),
            dma((2, to_right, pieces)), dma((2, to_right, pieces)),
            dma((2, peers)), dma((2, peers)), dma((DQ,)), dma((DQ,)),
        ],
        compiler_params=pltpu.CompilerParams(
            collective_id=0, has_side_effects=True, vmem_limit_bytes=56 * 1024 * 1024
        ),
    )(*operands)
    gi, gg, gu, gd = pl.pallas_call(
        hand_on,
        grid=(1,),
        out_shape=tuple(
            jax.ShapeDtypeStruct(dims, BF16) for dims in ((TOK, width),) + outs[1:]
        ),
        in_specs=[whole(outs[0]), hbm, hbm, hbm],
        out_specs=(whole((TOK, width)), hbm, hbm, hbm),
        scratch_shapes=[pltpu.VMEM(dims, BF16) for dims in outs[1:]] + [dma((2, 3))],
        compiler_params=pltpu.CompilerParams(vmem_limit_bytes=56 * 1024 * 1024),
    )(*results)
    return gi, gg[None], gu[None], gd[None]


def solution(mesh):
    rows = P(("node", "local"), None)
    blocks = P(("node", "local"), None, None)
    shape = (mesh.shape["node"], mesh.shape["local"])
    return jax.shard_map(
        functools.partial(on_device, shape),
        mesh=mesh,
        in_specs=(rows,) * 5 + (blocks,) * 3,
        out_specs=(rows,) + (blocks,) * 3,
        check_vma=False,
    )
```

time: 615 us -> 158 us (0.26)
  waiting for transfers between devices: 398 us -> 0 us
  Pallas kernels: 0 us -> 157 us
  blocking collectives: 122 us -> 0 us
  starting transfers between devices: 53.2 us -> 0 us
  between operations: 14.8 us -> 0.64 us
  matrix products: 13.9 us -> 0 us
  local copies, waits for them, and re-layouts: 7.18 us -> 0 us
    pallas_call x0 -> x2, Pallas kernels: none -> 157 us  [the longest x1 154 us: on_device(): pl.pallas_call(functools.partial(kernel, nx, ny, nq), grid=(1,), out_shap...]
    all_gather x2 -> x0, waiting for transfers between devices: 151 us -> none  [the longest x1 81.6 us: on_device(): lax.all_gather(inputs, 'node', axis=0, tiled=True)]
    unnamed x4 -> x0, waiting for transfers between devices: 138 us -> none
    all_to_all x2 -> x0, waiting for transfers between devices: 106 us -> none  [the longest x1 92.7 us: on_device(): lax.all_to_all(quarter_rows(slot_input, local_count), 'local', split_axis...]
    all_to_all x1 -> x0, blocking collectives: 103 us -> none  [on_device(): lax.all_to_all(input_part, 'local', split_axis=0, concat_axis=0, tiled=True)]
    all_to_all x2 -> x0, starting transfers between devices: 36.9 us -> none  [the longest x1 24.9 us: on_device(): lax.all_to_all(quarter_rows(slot_grad, local_count), 'local', split_axis=...]
    all_gather x1 -> x0, blocking collectives: 18.9 us -> none  [on_device(): lax.all_gather(window, 'node', axis=0, tiled=True)]
    ppermute x6 -> x0, starting transfers between devices: 16.2 us -> none  [partner_2(): return lax.ppermute(block, axis, route)]
  transfers between devices with their start and end apart: 11 -> 0, of which waited for: 6 -> 0; matrix products, arithmetic and copies ran while one was open for 2% -> 0% of each run, Pallas kernels for 0% -> 0%
where the time goes in v1:
time: 158 us
  Pallas kernels  157 us (99%)
    pallas_call x1, Pallas kernels, on_device(): pl.pallas_call(functools.partial(kernel, nx, ny, nq), grid=(1,), out_shap...  154 us
    pallas_call x1, Pallas kernels, on_device(): pl.pallas_call(hand_on, grid=(1,), out_shape=tuple((jax.ShapeDtypeStruct(...  3.68 us

profile of v1, /device:TPU:1, one launch (start us, length us, event | category | flops | bytes accessed | tf_op | source)
XLA Modules:
  0.0 158.0 jit_solution(18227114657555147615)
XLA Ops:
  0.6 153.7 %shard_map.111 = (bf16[4,16,896]{2,1,0:T(8,128)(2,1)}, bf16[1792,128]{1,0:T(8,128)(2,1)}, bf16[1792,128]{1,0:T(8,128)(2,1)}, bf16[128,1792]{1,0:T(8,128)(2,1)}) custom-call(bf16[8,7168]{1,0:T(8,128)(2,1)} %grad_ref.1, bf16[8,7168]{1,0:T(8,128)(2,1)} %inp_ref.1, s32[4,8]{1,0:T(4,128)} %bitcast.11, s32[4,8]{1,0:T(4,128)} %bitcast.12, bf16[8,8]{1,0:T(8,128)(2,1)} %comb_ref.1, ...), custom_call_target="tpu_custom_call" | custom-call | tf_op jit(solution)/shard_map/pallas_call | solution.py:527
  154.3 3.7 %shard_map.112 = (bf16[8,7168]{1,0:T(8,128)(2,1)}, bf16[1792,128]{1,0:T(8,128)(2,1)}, bf16[1792,128]{1,0:T(8,128)(2,1)}, bf16[128,1792]{1,0:T(8,128)(2,1)}) custom-call(bf16[4,16,896]{2,1,0:T(8,128)(2,1)} %get-tuple-element.12.fin, bf16[1792,128]{1,0:T(8,128)(2,1)} %get-tuple-element.13.gg, bf16[1792,128]{1,0:T(8,128)(2,1)} %get-tuple-element.14.gu, ...), custom_call_target="tpu_custom_call" | custom-call | tf_op jit(solution)/shard_map/pallas_call | solution.py:569

commit v2 on v1

--- a/solution.py
+++ b/solution.py
@@ -15,9 +15,9 @@
 ROWS = DQ * CAPE
 LANES = 128
 GROUPS = 16
-LAG = 1
-AHEAD = 4
+START = (0, 0, 0, 0)
 AG_JUMP = (0, 0, 0, 0)
+SPLIT = 1
 RS_JUMP = 3
 MESH = pl.DeviceIdType.MESH
 F32 = jnp.float32
@@ -64,7 +64,7 @@
 
 def pieces_of(half):
     tiles = half // LANES
-    lead = (tiles + 1) // 2
+    lead = (tiles + 1) // 2 if SPLIT else tiles
     out = []
     for h in range(2):
         out.append((h, h * half, lead * LANES))
@@ -77,11 +77,11 @@
     nx, ny, nq,
     grad_ref, inp_ref, gid_ref, code_ref, comb_ref, wg_ref, wu_ref, wd_ref,
     fin, gg_ref, gu_ref, gd_ref,
-    tok_out, tok, win, wts, packed, cnt, cnts, arrived, xs, dys, wgu,
-    mine, part, quad_in, hgrad, hpart, hquad_in, hid, back,
+    tok_out, tok, win, wts, packed, cnt, cnts, arrived, turned, landed, xs, dys, wgu,
+    mine, part, core_in, chip_out, chip_in, hid, back,
     summed, leaves, relay, allrelay, fin_out,
-    tok_send, tok_recv, win_send, win_recv, pack_send, pack_recv, cnt_send, cnt_recv,
-    ag_send, ag_recv, mid_send, mid_recv, hid_send, hid_recv,
+    tok_send, tok_recv, win_send, win_recv, along_send, along_recv, across_send, across_recv, cnt_send, cnt_recv,
+    ag_send, ag_recv, mid_send, mid_recv,
     rs_send, rs_recv, rel_send, rel_recv, fin_send, fin_recv,
 ):
     nodes = nx * ny
@@ -193,8 +193,13 @@
     below = one((row >> 3 == col >> 3) & (row < col))
     row, col = grid_of(cols, slots)
     tally = one((((row >> 3) & 1) == 0) & (row >> 4 == (col >> 2) & 3) & (col >> 4 == me_n))
+    fold = nx.bit_length() - 1
+
+    def group_at(order, u):
+        return u if order == 0 else ((u & (nx - 1)) << fold) + (u >> fold)
+
     row, col = grid_of(slots, GROUPS)
-    of_group = one(row >> 4 == col)
+    of_group = [one(group_at(order, row >> 4) == col) for order in range(2)]
     row, col = grid_of(GROUPS, slots)
     group_of = one(row == col >> 4)
     row, col = grid_of(slots, slots)
@@ -217,48 +222,58 @@
     def cnt_copy(k, slot):
         return copy(cnt, cnts.at[slot], cnt_send.at[k], cnt_recv.at[k], (node_to(k), me_l))
 
-    def pack_copy(c, k, slot):
+    at_xy = (my_x, my_y)
+
+    def node_on(axis, t):
+        return t * ny + my_y if axis == 0 else my_x * ny + t
+
+    def along_copy(c, k, slot):
+        axis = c % 2
+        t = lax.rem(at_xy[axis] + k, nx)
         return copy(
-            packed.at[c, node_to(k)], arrived.at[c, slot], pack_send.at[c, k], pack_recv.at[c, k],
-            (node_to(k), me_l),
-        )
-
-    w_at = dot(of_group, weights.astype(BF16))
-    r_at = dot(of_group, ranks.astype(BF16))
+            packed.at[c, pl.ds(t * nx, nx)], arrived.at[c, slot],
+            along_send.at[c, k], along_recv.at[c, k], (node_on(axis, t), me_l),
+        )
+
+    def across_copy(c, k, slot):
+        axis = 1 - c % 2
+        t = lax.rem(at_xy[axis] + k, nx)
+        return copy(
+            turned.at[c, t], landed.at[c, slot],
+            across_send.at[c, k], across_recv.at[c, k], (node_on(axis, t), me_l),
+        )
+
+    picks = []
     row, col = grid_of(slots, cols)
-    fits = ((row >> 2) & 3) == col >> 4
-    fits = fits & (r_at == (row & 3).astype(F32)) & (w_at > 0)
     is_grad = ((col >> 3) & 1) == 1
-    picks = [
-        one(fits & jnp.logical_not(is_grad)),
-        jnp.where(fits & is_grad, w_at, 0.0).astype(BF16),
-    ]
+    for order in range(2):
+        w_at = dot(of_group[order], weights.astype(BF16))
+        r_at = dot(of_group[order], ranks.astype(BF16))
+        fits = ((row >> 2) & 3) == col >> 4
+        fits = fits & (r_at == (row & 3).astype(F32)) & (w_at > 0)
+        picks.append((
+            one(fits & jnp.logical_not(is_grad)),
+            jnp.where(fits & is_grad, w_at, 0.0).astype(BF16),
+        ))
 
     def pack(c):
         a, h = c // 2, c % 2
-        rows = dot(picks[a], tok[h].reshape(cols, half))
+        mine_at = at_xy[c % 2]
+        rows = dot(picks[c % 2][a], tok[h].reshape(cols, half))
         packed[c] = rows.astype(BF16).reshape(nodes, ROWS, half)
-        arrived[c, me_n] = packed[c, me_n]
-
-    def pack_go(c):
-        for k in peers:
-            go(pack_copy(c, k, me_n))
+        for k in range(1, nx):
+            go(along_copy(c, k, mine_at))
+        arrived[c, mine_at] = packed[c, pl.ds(mine_at * nx, nx)]
 
     for d in mates:
         tok_copy(d, 0, mate(d)).wait_recv()
     pack(0)
-    pack_go(0)
     for k in peers:
         go(cnt_copy(k, me_n))
     cnts[me_n] = cnt[...]
     for d in mates:
         tok_copy(d, 1, mate(d)).wait_recv()
-    pack(1)
-    for c in range(1, AHEAD):
-        if c > 1:
-            pack(c)
-        pack_go(c)
-    for c in range(max(2, AHEAD), 4):
+    for c in range(1, 4):
         pack(c)
 
     for k in peers:
@@ -267,17 +282,50 @@
     for m in range(nodes):
         counts = counts + cnts[m].astype(F32)
     begin = dot(counts.astype(BF16), before).astype(BF16)
-    row, col = grid_of(ROWS, GROUPS)
-    start = dot(one(col == me_n), begin)
-    row, col = grid_of(ROWS, slots)
-    merge = one(
-        (row >> 2 == (col >> 2) & 3) & ((row & 3).astype(F32) == start + (col & 3).astype(F32))
-    )
+    line = nx * ROWS
+    merges = []
+    for order in range(2):
+        row, col = grid_of(line, GROUPS)
+        group = my_x * ny + (row >> 4) if order == 0 else (row >> 4) * ny + my_y
+        start = dot(one(group == col), begin).astype(BF16)
+        row, col = grid_of(slots, slots)
+        source = node_on(order, col >> (4 + fold))
+        start = dot(
+            start,
+            one((row >> 4 == source) & ((row & 3) == 0) & ((row >> 2) & 3 == (col >> 2) & 3)),
+        )
+        row, col = grid_of(line, slots)
+        same = (row >> 4 == (col >> 4) & (nx - 1)) & ((row >> 2) & 3 == (col >> 2) & 3)
+        merges.append(one(same & ((row & 3).astype(F32) == start + (col & 3).astype(F32))))
     place = jnp.where(weights > 0, ranks + dot(begin, own_base), 255.0)
     place = dot(place.astype(BF16), group_of, FIRST)
     row, col = grid_of(cols, slots)
     stands = (row >> 4 == (col >> 2) & 3) & (place == (col & 3).astype(F32))
     collect = [one(stands & (((row >> 3) & 1) == h)) for h in range(2)]
+
+    def turn_off(c):
+        axis = c % 2
+        for k in range(1, nx):
+            along_copy(c, k, lax.rem(at_xy[axis] + nx - k, nx)).wait_recv()
+        rows = dot(merges[axis], arrived[c].reshape(slots, half))
+        turned[c] = rows.astype(BF16).reshape(nx, ROWS, half)
+        here = at_xy[1 - axis]
+        for k in range(1, nx):
+            go(across_copy(c, k, here))
+        landed[c, here] = turned[c, here]
+
+    def land(c):
+        here = at_xy[1 - c % 2]
+        for k in range(1, nx):
+            across_copy(c, k, lax.rem(here + nx - k, nx)).wait_recv()
+        total = landed[c, 0].astype(F32)
+        for k in range(1, nx):
+            total = total + landed[c, k].astype(F32)
+        rings[c // 2][0:ROWS, (c % 2) * half:(c % 2 + 1) * half] = total.astype(BF16)
+
+    for c in range(4):
+        if START[c] == 0:
+            turn_off(c)
 
     rings = (xs, dys)
 
@@ -301,59 +349,28 @@
             block(c, dst), block(c, dst), ag_send.at[c, dst], ag_recv.at[c, dst], quad_at(1)
         ).wait_recv()
 
-    share = nq * ROWS // DQ
-
-    def rows_at(ref, owner, at, width):
-        return ref.at[pl.ds(pl.multiple_of(owner * share, share), share), pl.ds(at, width)]
-
-    def own_rows(ref):
-        return ref[pl.ds(pl.multiple_of(b * share, share), share), :]
-
-    def mid_copy(d):
-        return copy(
-            rows_at(part, mate(d), 0, 2 * hw), quad_in.at[d - 1],
-            mid_send.at[0, d], mid_recv.at[0, d], in_quad(d),
-        )
-
-    def hgrad_copy(d):
-        return copy(
-            rows_at(hpart, mate(d), 0, hw), hquad_in.at[d - 1],
-            mid_send.at[1, d], mid_recv.at[1, d], in_quad(d),
-        )
-
     whole = set()
 
     def after_chunk(c):
         span = slice((c % 2) * half, (c % 2 + 1) * half)
+        if c // 2 == 0:
+            total, at = dot(xs[:, span], wgu[span, :]), slice(0, 2 * hw)
+        else:
+            total, at = dot(dys[:, span], wd_ref[:, span], LAST), slice(2 * hw, 3 * hw)
+        if c ^ 1 in whole:
+            total = mine[:, at] + total
+        mine[:, at] = total
         whole.add(c)
-        a = c // 2
-        if a == 0:
-            total = dot(xs[:, span], wgu[span, :])
-        else:
-            total = dot(dys[:, span], wd_ref[:, span], LAST)
-        both = {2 * a, 2 * a + 1} <= whole
-        keep, send, move = ((mine, part, mid_copy), (hgrad, hpart, hgrad_copy))[a]
-        if both:
-            total = keep[...] + total
-            send[...] = total.astype(BF16)
-            for d in mates:
-                go(move(d))
-        keep[...] = total
 
     last = [max(route.last() for route in routes) for routes in ag_routes]
-    for turn in range(max(last[c] + LAG * c for c in range(4)) + 1):
+    for turn in range(max(last[c] + START[c] for c in range(4)) + 1):
         for c in range(4):
-            step = turn - LAG * c
+            step = turn - START[c]
             if step == 0:
-                for k in peers:
-                    pack_copy(c, k, node_from(k)).wait_recv()
-                merged = dot(merge, arrived[c].reshape(slots, half)).astype(BF16)
-                rings[c // 2][0:ROWS, (c % 2) * half:(c % 2 + 1) * half] = merged
+                land(c)
                 for way in range(2):
                     for i in reversed(ag_routes[c][way].children(0)):
                         go(ag_copy(c, way, i))
-                if c + AHEAD < 4:
-                    pack_go(c + AHEAD)
             for way in range(2):
                 route = ag_routes[c][way]
                 for i in range(route.far, 0, -1):
@@ -363,35 +380,43 @@
                             go(ag_copy(c, way, j))
             if step == last[c]:
                 after_chunk(c)
-
-    total = own_rows(mine)
-    for d in mates:
-        mid_copy(d).wait_recv()
-        total = total + quad_in[d - 1].astype(F32)
-    gate_pre, up_pre = total[:, :hw], total[:, hw:]
+        for c in range(4):
+            if START[c] == turn + 1:
+                turn_off(c)
+
+    core = lax.bitwise_and(b, 1)
+    some = nq * ROWS // 2
+
+    def rows_of(ref, owner):
+        return ref.at[pl.ds(pl.multiple_of(owner * some, some), some)]
+
+    def core_copy():
+        return copy(part, core_in, mid_send.at[0], mid_recv.at[0], in_quad(1))
+
+    def chip_copy():
+        return copy(chip_out, rows_of(chip_in, core), mid_send.at[1], mid_recv.at[1], in_quad(2))
+
+    def half_copy(owner):
+        rows = rows_of(chip_in, owner)
+        return copy(rows, rows, mid_send.at[2], mid_recv.at[2], in_quad(1))
+
+    part[...] = mine[...].astype(BF16)
+    go(core_copy())
+    core_copy().wait_recv()
+    mine[...] = mine[...] + core_in[...].astype(F32)
+    chip_out[...] = mine[pl.ds(pl.multiple_of(core * some, some), some), :].astype(BF16)
+    go(chip_copy())
+    chip_copy().wait_recv()
+    go(half_copy(core))
+    half_copy(1 - core).wait_recv()
+    total = mine[...] + chip_in[...].astype(F32)
+    gate_pre, up_pre, hidden_grad = (total[:, i * hw:(i + 1) * hw] for i in range(3))
     sigmoid_gate = 1.0 / (1.0 + jnp.exp(-gate_pre))
     activated = gate_pre * sigmoid_gate
     slope = up_pre * sigmoid_gate * (1.0 + gate_pre * (1.0 - sigmoid_gate))
-    hidden_grad = own_rows(hgrad)
-    for d in mates:
-        hgrad_copy(d).wait_recv()
-        hidden_grad = hidden_grad + hquad_in[d - 1].astype(F32)
-    hid[pl.ds(pl.multiple_of(b * share, share), share), :] = jnp.concatenate(
-        [hidden_grad * slope, hidden_grad * activated, activated * up_pre], axis=1
-    ).astype(BF16)
-
-    def hid_copy(d, owner, i):
-        at, width = ((0, 2 * hw), (2 * hw, hw))[i]
-        return copy(
-            rows_at(hid, b, at, width), rows_at(hid, owner, at, width),
-            hid_send.at[i, d], hid_recv.at[i, d], in_quad(d),
-        )
-
-    for i in range(2):
-        for d in mates:
-            go(hid_copy(d, b, i))
-    for d in mates:
-        hid_copy(d, mate(d), 0).wait_recv()
+    hid[:, 0:hw] = (hidden_grad * slope).astype(BF16)
+    hid[:, hw:2 * hw] = (hidden_grad * activated).astype(BF16)
+    hid[:, 2 * hw:3 * hw] = (activated * up_pre).astype(BF16)
     deltas = hid[:, 0:2 * hw]
     back[...] = dot(deltas, wgu[...], LAST)
 
@@ -457,8 +482,6 @@
     grads = dot(xs[...], deltas, FIRST)
     gg_ref[...] = grads[:, :hw].astype(BF16)
     gu_ref[...] = grads[:, hw:].astype(BF16)
-    for d in mates:
-        hid_copy(d, mate(d), 1).wait_recv()
     gd_ref[...] = dot(hid[:, 2 * hw:3 * hw], dys[...], FIRST).astype(BF16)
 
     sums = jnp.zeros((cols, half), F32)
@@ -538,16 +561,17 @@
             pltpu.VMEM((4, nodes, ROWS, half), BF16),
             pltpu.VMEM((GROUPS, slots), BF16),
             pltpu.VMEM((nodes, GROUPS, slots), BF16),
-            pltpu.VMEM((4, nodes, ROWS, half), BF16),
+            pltpu.VMEM((4, nx, nx, ROWS, half), BF16),
+            pltpu.VMEM((4, nx, ROWS, half), BF16),
+            pltpu.VMEM((4, nx, ROWS, half), BF16),
             pltpu.VMEM((ring, feat), BF16),
             pltpu.VMEM((ring, feat), BF16),
             pltpu.VMEM((feat, 2 * hw), BF16),
-            pltpu.VMEM((ring, 2 * hw), F32),
-            pltpu.VMEM((ring, 2 * hw), BF16),
-            pltpu.VMEM((DQ - 1, ring // DQ, 2 * hw), BF16),
-            pltpu.VMEM((ring, hw), F32),
-            pltpu.VMEM((ring, hw), BF16),
-            pltpu.VMEM((DQ - 1, ring // DQ, hw), BF16),
+            pltpu.VMEM((ring, 3 * hw), F32),
+            pltpu.VMEM((ring, 3 * hw), BF16),
+            pltpu.VMEM((ring, 3 * hw), BF16),
+            pltpu.VMEM((ring // 2, 3 * hw), BF16),
+            pltpu.VMEM((ring, 3 * hw), BF16),
             pltpu.VMEM((ring, 3 * hw), BF16),
             pltpu.VMEM((ring, feat), F32),
             pltpu.VMEM((2, to_right + 1, ROWS, feat), BF16),
@@ -556,9 +580,10 @@
             pltpu.VMEM((2, nodes, ROWS, half), BF16),
             pltpu.VMEM((DQ, 2 * TOK, half), BF16),
             dma((2, DQ)), dma((2, DQ)), dma((DQ,)), dma((DQ,)),
-            dma((4, peers)), dma((4, peers)), dma((peers,)), dma((peers,)),
+            dma((4, nx)), dma((4, nx)), dma((4, nx)), dma((4, nx)),
+            dma((peers,)), dma((peers,)),
             dma((4, nq)), dma((4, nq)),
-            dma((2, DQ)), dma((2, DQ)), dma((2, DQ)), dma((2, DQ)),
+            dma((3,)), dma((3,)),
             dma((2, to_right, pieces)), dma((2, to_right, pieces)),
             dma((2, peers)), dma((2, peers)), dma((DQ,)), dma((DQ,)),
         ],

time: 158 us -> 148 us (0.937)
  Pallas kernels: 157 us -> 147 us
    pallas_call x1, Pallas kernels: 154 us -> 143 us  [on_device(): pl.pallas_call(functools.partial(kernel, nx, ny, nq), grid=(1,), out_shap...]
where the time goes in v2:
time: 148 us
  Pallas kernels  147 us (99%)
    pallas_call x1, Pallas kernels, on_device(): pl.pallas_call(functools.partial(kernel, nx, ny, nq), grid=(1,), out_shap...  143 us
    pallas_call x1, Pallas kernels, on_device(): pl.pallas_call(hand_on, grid=(1,), out_shape=tuple((jax.ShapeDtypeStruct(...  3.68 us

profile of v2, /device:TPU:1, one launch (start us, length us, event | category | flops | bytes accessed | tf_op | source)
XLA Modules:
  0.0 147.6 jit_solution(5890465289435719406)
XLA Ops:
  0.6 143.3 %shard_map.111 = (bf16[4,16,896]{2,1,0:T(8,128)(2,1)}, bf16[1792,128]{1,0:T(8,128)(2,1)}, bf16[1792,128]{1,0:T(8,128)(2,1)}, bf16[128,1792]{1,0:T(8,128)(2,1)}) custom-call(bf16[8,7168]{1,0:T(8,128)(2,1)} %grad_ref.1, bf16[8,7168]{1,0:T(8,128)(2,1)} %inp_ref.1, s32[4,8]{1,0:T(4,128)} %bitcast.11, s32[4,8]{1,0:T(4,128)} %bitcast.12, bf16[8,8]{1,0:T(8,128)(2,1)} %comb_ref.1, ...), custom_call_target="tpu_custom_call" | custom-call | tf_op jit(solution)/shard_map/pallas_call | solution.py:550
  143.9 3.7 %shard_map.112 = (bf16[8,7168]{1,0:T(8,128)(2,1)}, bf16[1792,128]{1,0:T(8,128)(2,1)}, bf16[1792,128]{1,0:T(8,128)(2,1)}, bf16[128,1792]{1,0:T(8,128)(2,1)}) custom-call(bf16[4,16,896]{2,1,0:T(8,128)(2,1)} %get-tuple-element.12.fin, bf16[1792,128]{1,0:T(8,128)(2,1)} %get-tuple-element.13.gg, bf16[1792,128]{1,0:T(8,128)(2,1)} %get-tuple-element.14.gu, ...), custom_call_target="tpu_custom_call" | custom-call | tf_op jit(solution)/shard_map/pallas_call | solution.py:594

commit v3 on v2

--- a/solution.py
+++ b/solution.py
@@ -76,8 +76,8 @@
 def kernel(
     nx, ny, nq,
     grad_ref, inp_ref, gid_ref, code_ref, comb_ref, wg_ref, wu_ref, wd_ref,
-    fin, gg_ref, gu_ref, gd_ref,
-    tok_out, tok, win, wts, packed, cnt, cnts, arrived, turned, landed, xs, dys, wgu,
+    fin, gg_out, gu_out, gd_out,
+    gg_ref, gu_ref, gd_ref, wd_in, own_sem, tok_out, tok, win, wts, packed, cnt, cnts, arrived, turned, landed, xs, dys, wgu,
     mine, part, core_in, chip_out, chip_in, hid, back,
     summed, leaves, relay, allrelay, fin_out,
     tok_send, tok_recv, win_send, win_recv, along_send, along_recv, across_send, across_recv, cnt_send, cnt_recv,
@@ -85,8 +85,7 @@
     rs_send, rs_recv, rel_send, rel_recv, fin_send, fin_recv,
 ):
     nodes = nx * ny
-    feat = wg_ref.shape[0]
-    hw = wg_ref.shape[1]
+    feat, hw = wg_ref.shape
     half = feat // 2
     slots = nodes * ROWS
     to_right = nq // 2
@@ -144,6 +143,14 @@
     greet += [quad_at(k) for k in sorted(apart)]
     for device in greet:
         pl.semaphore_signal(barrier, inc=1, device_id=device, device_id_type=MESH)
+
+    loads = [
+        pltpu.make_async_copy(wg_ref, wgu.at[:, pl.ds(0, hw)], own_sem.at[0]),
+        pltpu.make_async_copy(wu_ref, wgu.at[:, pl.ds(hw, hw)], own_sem.at[1]),
+        pltpu.make_async_copy(wd_ref, wd_in, own_sem.at[2]),
+    ]
+    for c in loads:
+        c.start()
 
     for q in range(DQ):
         for h in range(2):
@@ -206,8 +213,6 @@
     before = one((row >> 4 < col >> 4) & ((row & 15) == (col & 15)))
     row, col = grid_of(slots, cols)
     own_base = one((row >> 4 == me_n) & ((row & 3) == 0) & (((row >> 2) & 3) == col >> 4))
-    wgu[:, 0:hw] = wg_ref[...]
-    wgu[:, hw:2 * hw] = wu_ref[...]
 
     for d in mates:
         win_copy(d, mate(d)).wait_recv()
@@ -326,6 +331,8 @@
     for c in range(4):
         if START[c] == 0:
             turn_off(c)
+    for c in loads:
+        c.wait()
 
     rings = (xs, dys)
 
@@ -356,7 +363,7 @@
         if c // 2 == 0:
             total, at = dot(xs[:, span], wgu[span, :]), slice(0, 2 * hw)
         else:
-            total, at = dot(dys[:, span], wd_ref[:, span], LAST), slice(2 * hw, 3 * hw)
+            total, at = dot(dys[:, span], wd_in[:, span], LAST), slice(2 * hw, 3 * hw)
         if c ^ 1 in whole:
             total = mine[:, at] + total
         mine[:, at] = total
@@ -483,6 +490,13 @@
     gg_ref[...] = grads[:, :hw].astype(BF16)
     gu_ref[...] = grads[:, hw:].astype(BF16)
     gd_ref[...] = dot(hid[:, 2 * hw:3 * hw], dys[...], FIRST).astype(BF16)
+    stores = [
+        pltpu.make_async_copy(gg_ref, gg_out, own_sem.at[3]),
+        pltpu.make_async_copy(gu_ref, gu_out, own_sem.at[4]),
+        pltpu.make_async_copy(gd_ref, gd_out, own_sem.at[5]),
+    ]
+    for c in stores:
+        c.start()
 
     sums = jnp.zeros((cols, half), F32)
     for h in range(2):
@@ -501,6 +515,8 @@
     fin[b] = fin_out[b]
     for d in mates:
         fin_copy(d, mate(d)).wait_recv()
+    for c in stores:
+        c.wait()
     for c in started:
         c.wait_send()
 
@@ -551,9 +567,10 @@
         functools.partial(kernel, nx, ny, nq),
         grid=(1,),
         out_shape=tuple(jax.ShapeDtypeStruct(dims, BF16) for dims in outs),
-        in_specs=[whole(o.shape) for o in operands],
-        out_specs=tuple(whole(dims) for dims in outs),
-        scratch_shapes=[
+        in_specs=[whole(o.shape) for o in operands[:5]] + [hbm] * 3,
+        out_specs=(whole(outs[0]), hbm, hbm, hbm),
+        scratch_shapes=[pltpu.VMEM(dims, BF16) for dims in outs[1:] + outs[3:]] + [
+            dma((6,)),
             pltpu.VMEM((2, DQ, 2 * TOK, half), BF16),
             pltpu.VMEM((2, DQ, 2 * TOK, half), BF16),
             pltpu.VMEM((GROUPS, LANES), F32),

time: 148 us -> 147 us (level)
  Pallas kernels: 147 us -> 145 us
    pallas_call x1, Pallas kernels: 143 us -> 142 us  [on_device(): pl.pallas_call(functools.partial(kernel, nx, ny, nq), grid=(1,), out_shap...]
where the time goes in v3:
time: 147 us; the launch traced here: 146 us
  Pallas kernels  145 us (99%)
    pallas_call x1, Pallas kernels, on_device(): pl.pallas_call(functools.partial(kernel, nx, ny, nq), grid=(1,), out_shap...  142 us
    pallas_call x1, Pallas kernels, on_device(): pl.pallas_call(hand_on, grid=(1,), out_shape=tuple((jax.ShapeDtypeStruct(...  3.68 us

profile of v3, /device:TPU:1, one launch (start us, length us, event | category | flops | bytes accessed | tf_op | source)
XLA Modules:
  0.0 146.0 jit_solution(15191429492545272072)
XLA Ops:
  0.6 141.7 %shard_map.111 = (bf16[4,16,896]{2,1,0:T(8,128)(2,1)}, bf16[1792,128]{1,0:T(8,128)(2,1)}, bf16[1792,128]{1,0:T(8,128)(2,1)}, bf16[128,1792]{1,0:T(8,128)(2,1)}) custom-call(bf16[8,7168]{1,0:T(8,128)(2,1)} %grad_ref.1, bf16[8,7168]{1,0:T(8,128)(2,1)} %inp_ref.1, s32[4,8]{1,0:T(4,128)} %bitcast.11, s32[4,8]{1,0:T(4,128)} %bitcast.12, bf16[8,8]{1,0:T(8,128)(2,1)} %comb_ref.1, ...), custom_call_target="tpu_custom_call" | custom-call | tf_op jit(solution)/shard_map/pallas_call | solution.py:566
  142.4 3.7 %shard_map.112 = (bf16[8,7168]{1,0:T(8,128)(2,1)}, bf16[1792,128]{1,0:T(8,128)(2,1)}, bf16[1792,128]{1,0:T(8,128)(2,1)}, bf16[128,1792]{1,0:T(8,128)(2,1)}) custom-call(bf16[4,16,896]{2,1,0:T(8,128)(2,1)} %get-tuple-element.12.fin, bf16[1792,128]{1,0:T(8,128)(2,1)} %get-tuple-element.13.gg, bf16[1792,128]{1,0:T(8,128)(2,1)} %get-tuple-element.14.gu, ...), custom_call_target="tpu_custom_call" | custom-call | tf_op jit(solution)/shard_map/pallas_call | solution.py:611
